TPU v7x, 32 devices: a whole 2x2x4 slice. The times are simulated.
32 devices in a mesh: grp: 2 (over y), wide: 4 (over z), narrow: 4 (over x, core).
Axes of the slice: x: 2, y: 2, z: 4, core: 2. Of those that a mesh axis runs over, the one named last changes fastest.
Arguments:
- hidden_in: bfloat16 [384, 16384], P(('grp', 'wide'), 'narrow'), parts along dimension 0, may hold values from -240 to 240
- norm_gain: float32 [16384], P('narrow'), may hold values from 0.1 to 1.9
- query_weight: bfloat16 [16384, 16384], P('narrow', 'wide'), may hold values from -0.046875 to 0.046875
- key_weight: bfloat16 [16384, 1024], P('narrow', 'wide'), may hold values from -0.046875 to 0.046875
- value_weight: bfloat16 [16384, 1024], P('narrow', 'wide'), may hold values from -0.046875 to 0.046875
- positions: int32 [384], P(('grp', 'narrow')), parts along dimension 0, may hold values from 0 to 8191
Outputs:
- queries: bfloat16 [384, 16384], P(('grp', 'narrow'), 'wide'), parts along dimension 0
- keys_new: bfloat16 [384, 1024], P(('grp', 'narrow'), 'wide'), parts along dimension 0
- values_new: bfloat16 [384, 1024], P(('grp', 'narrow'), 'wide'), parts along dimension 0
There are 2 independent parts, one for each index of `grp`. A program takes and returns all parts, laid end to end along the dimension named above; an argument that names none is the same for every part. Nothing has to cross between parts.
All inputs are finite; a program needn't handle non-finite values.
Results may differ from a plain program's by a relative error of at most 0.005.
Values may be sent and summed in bfloat16 or wider, within the bound.
A program may use at most 128 MiB of HBM per device.

v0:
```python
import math

import jax
import jax.numpy as jnp
from jax import lax
from jax.sharding import PartitionSpec as P

D = 16384
HEAD_DIM = 128


def frequency(pair_index, head_dim):
    base = jnp.float32(500000.0) ** (-2.0 * pair_index / jnp.float32(head_dim))
    wavelen = 2.0 * math.pi / base
    smooth = (8192.0 / wavelen - 1.0) / 3.0
    middle = (1.0 - smooth) * base / 8.0 + smooth * base
    return jnp.where(wavelen < 2048.0, base, jnp.where(wavelen > 8192.0, base / 8.0, middle))


def rotate(block, positions, offset):
    count, width = block.shape
    pairs = block.reshape(count, width // 2, 2)
    first = pairs[:, :, 0]
    second = pairs[:, :, 1]
    columns = offset + 2 * jnp.arange(width // 2, dtype=jnp.int32)
    pair_index = (columns % HEAD_DIM // 2).astype(jnp.float32)
    angle = positions.astype(jnp.float32)[:, None] * frequency(pair_index, HEAD_DIM)[None, :]
    cosine = jnp.cos(angle)
    sine = jnp.sin(angle)
    turned = jnp.stack([first * cosine - second * sine, first * sine + second * cosine], axis=-1)
    return turned.reshape(count, width)


def shards(hidden_in, norm_gain, query_weight, key_weight, value_weight, positions):
    local_rows = hidden_in.shape[0]
    total_rows = local_rows * lax.axis_size("wide")
    own_rows = total_rows // lax.axis_size("narrow")
    row_start = lax.axis_index("narrow") * own_rows
    query_cols = query_weight.shape[1]
    key_cols = key_weight.shape[1]
    joint_weight = jnp.concatenate([key_weight, value_weight], axis=1)
    raw = lax.all_gather(hidden_in, "wide", axis=0, tiled=True).astype(jnp.float32)
    scaled = (raw * norm_gain[None, :]).astype(jnp.bfloat16)
    part_q = jnp.dot(scaled, query_weight, preferred_element_type=jnp.float32)
    part_kv = jnp.dot(scaled, joint_weight, preferred_element_type=jnp.float32)
    part_sq = jnp.sum(raw * raw, axis=1)
    squares_all = lax.psum(part_sq, "narrow")
    mine_q, mine_kv = (
        lax.psum_scatter(part_q, "narrow", scatter_dimension=0, tiled=True),
        lax.psum_scatter(part_kv, "narrow", scatter_dimension=0, tiled=True),
    )
    mine_sq = lax.dynamic_slice_in_dim(squares_all, row_start, own_rows, 0)
    inverse = lax.rsqrt(mine_sq / D + 1e-05)[:, None]
    column_q = lax.axis_index("wide") * query_cols
    column_k = lax.axis_index("wide") * key_cols
    queries = rotate(mine_q * inverse, positions, column_q).astype(jnp.bfloat16)
    keys_new = rotate(mine_kv[:, :key_cols] * inverse, positions, column_k).astype(jnp.bfloat16)
    values_new = (mine_kv[:, key_cols:] * inverse).astype(jnp.bfloat16)
    return (queries, keys_new, values_new)


def solution(mesh):
    return jax.shard_map(
        shards,
        mesh=mesh,
        in_specs=(
            P(("grp", "wide"), "narrow"),
            P("narrow"),
            P("narrow", "wide"),
            P("narrow", "wide"),
            P("narrow", "wide"),
            P(("grp", "narrow")),
        ),
        out_specs=(
            P(("grp", "narrow"), "wide"),
            P(("grp", "narrow"), "wide"),
            P(("grp", "narrow"), "wide"),
        ),
        check_vma=False,
    )
```

profile of v0, /device:TPU:0, one launch (start us, length us, event | category | flops | bytes accessed | tf_op | source)
XLA Modules:
  0.0 131.6 jit_solution(7886914073637513930)
XLA Ops:
  7.2 0.0 all-gather.2.cloned.1.call-start
  7.2 0.7 all-gather.2.cloned.1.call-update
  7.9 0.0 copy-start.1
  7.9 0.0 reduce-scatter.5.cloned.1.call-start
  8.0 41.4 %all-gather.2.cloned.1.call-done = bf16[192,4096]{1,0:T(8,128)(2,1)} async-done(((bf16[48,4096]{1,0:T(8,128)(2,1)}), bf16[192,4096]{1,0:T(8,128)(2,1)}) %all-gather.2.cloned.1.call-update) | async-done | bytes 1572880 | tf_op jit(solution)/shard_map/all_gather | solution.py:42
  49.4 0.0 copy-start
  49.4 4.6 %fusion = f32[192,512]{1,0:T(8,128)} fusion(bf16[4096,256]{1,0:T(8,128)(2,1)} %param.10, bf16[4096,256]{1,0:T(8,128)(2,1)} %param.9, bf16[192,4096]{1,0:T(8,128)(2,1)} %all-gather.2.cloned.1.call-done, f32[4096]{0:T(1024)} %param.7), kind=kOutput, calls=%fused_computation | convolution fusion | flops 816054272 | bytes 6176768 | tf_op jit(solution)/shard_map/dot_general | solution.py:45
  54.0 0.0 reduce-scatter.5.cloned.1.call-update
  54.0 0.0 reduce-scatter.3.cloned.1.call-start
  54.0 0.0 copy-done.1
  54.0 0.0 copy-done
  54.0 15.9 %fusion.7 = f32[192,4096]{1,0:T(8,128)} fusion(bf16[4096,4096]{1,0:T(8,128)(2,1)} %param.8, bf16[192,4096]{1,0:T(8,128)(2,1)S(1)} %copy-done, f32[4096]{0:T(1024)S(1)} %copy-done.1), kind=kOutput, calls=%fused_computation.8 | convolution fusion | flops 6444810240 | bytes 38289408 | tf_op jit(solution)/shard_map/dot_general | solution.py:44
  69.9 0.0 copy-start.2
  69.9 0.0 reduce-scatter.3.cloned.1.call-update
  70.0 0.6 copy-done.2
  70.7 0.4 fusion.5
  71.1 6.4 %psum.7 = f32[192]{0:T(256)S(1)} all-reduce(f32[192]{0:T(256)S(1)} %fusion.5), channel_id=1, replica_groups=mesh['grp'=2,'wide'=4,'narrow'=4] {'narrow'}, use_global_device_ids=true, to_apply=%region_2.0 | all-reduce | flops 192 | bytes 1536 | tf_op jit(solution)/shard_map/psum | solution.py:47
  77.5 0.1 add_rsqrt_fusion
  77.6 0.0 reduce-scatter.5.cloned.1.call-done
  77.6 1.5 %fusion.17 = (bf16[48,256]{1,0:T(8,128)(2,1)}, f32[48,256]{1,0:T(8,128)S(1)}) fusion(f32[48,512]{1,0:T(8,128)} %reduce-scatter.5.cloned.1.call-done, f32[48]{0:T(128)S(1)} %add_rsqrt_fusion), kind=kLoop, calls=%fused_computation.22 | loop fusion | flops 36864 | bytes 172224 | tf_op jit(solution)/shard_map/convert_element_type | solution.py:58
  79.1 0.1 copy.31
  79.2 0.1 fusion.36
  79.3 0.1 copy.39
  79.4 0.1 copy.40
  79.4 0.2 fusion.23
  79.7 0.1 copy.34
  79.8 0.7 copy.36
  80.5 33.9 %reduce-scatter.3.cloned.1.call-done = f32[48,4096]{1,0:T(8,128)} async-done(((f32[192,4096]{1,0:T(8,128)}), f32[48,4096]{1,0:T(8,128)}) %reduce-scatter.3.cloned.1.call-update) | async-done | bytes 786448 | tf_op jit(solution)/shard_map/reduce_scatter | solution.py:49
  114.4 1.3 broadcast_multiply_fusion
  115.6 0.6 copy.27
  116.2 2.4 %fusion.35 = (f32[48,2048,1]{0,2,1:T(1,128)S(1)}, f32[48,2048,1]{0,2,1:T(1,128)}) fusion(f32[48,2048,2]{0,2,1:T(2,128)S(1)} %bitcast.5), kind=kLoop, calls=%fused_computation.64 | loop fusion | bytes 1572864 | tf_op jit(solution)/shard_map/slice | solution.py:24
  118.7 2.3 %copy.37 = f32[48,2048,1]{1,0,2:T(8,128)S(1)} copy(f32[48,2048,1]{0,2,1:T(1,128)} %get-tuple-element.16) | data formatting | bytes 786432
  120.9 0.5 copy.38
  121.5 1.7 %fusion.14 = (bf16[48,2048,1]{1,0,2:T(8,128)(2,1)S(1)}, bf16[48,2048,1]{1,0,2:T(8,128)(2,1)S(1)}) fusion(f32[48,2048,1]{1,0,2:T(8,128)S(1)} %copy.38, f32[48,2048,1]{1,0,2:T(8,128)S(1)} %copy.37, f32[2048]{0:T(1024)S(1)} %select_select_fusion, f32[48]{0:T(128)S(1)} %convert_element_type.37), kind=kLoop, calls=%fused_computation.16 | loop fusion | flops 884736 | bytes 1188032 | tf_op jit(solution)/shard_map/convert.2
  123.3 0.8 copy.30
  124.0 1.1 copy.35
  (5 shorter events, 0.1 us)
Async XLA Ops:
  7.2 42.2 %all-gather.2.cloned.1.call-start = ((), (), s32[]{:S(2)}) async-start(), calls=%async_computation.2 | async-start | bytes 1966080 | tf_op jit(solution)/shard_map/all_gather | solution.py:42
  7.9 46.1 %copy-start.1 = (f32[4096]{0:T(1024)S(1)}, f32[4096]{0:T(1024)}, u32[]{:S(2)}) copy-start(f32[4096]{0:T(1024)} %param.7) | copy-start | bytes 49156
  7.9 69.7 %reduce-scatter.5.cloned.1.call-start = ((), (), s32[]{:S(2)}) async-start(), calls=%async_computation.4 | async-start | bytes 491520 | tf_op jit(solution)/shard_map/reduce_scatter | solution.py:50
  49.4 4.6 %copy-start = (bf16[192,4096]{1,0:T(8,128)(2,1)S(1)}, bf16[192,4096]{1,0:T(8,128)(2,1)}, u32[]{:S(2)}) copy-start(bf16[192,4096]{1,0:T(8,128)(2,1)} %all-gather.2.cloned.1.call-done) | copy-start | bytes 4718596
  54.0 60.4 %reduce-scatter.3.cloned.1.call-start = ((), (), s32[]{:S(2)}) async-start(), calls=%async_computation.3 | async-start | bytes 3932160 | tf_op jit(solution)/shard_map/reduce_scatter | solution.py:49
  69.9 0.7 copy-start.2
Sparse Core Ops, SparseCore 0:
  9.6 39.7 all-gather.1
  54.1 19.7 reduce-scatter.4
  76.4 37.9 reduce-scatter.2
where the time goes:
time: 132 us
  waiting for transfers between devices  76 us (58%)
  matrix products  20.4 us (15%)
  between operations  13.9 us (11%)
  local copies, waits for them, and re-layouts  9.47 us (7%)
  blocking collectives  6.44 us (5%)
  other arithmetic  5.28 us (4%)
    all_gather x1, waiting for transfers between devices, shards(): lax.all_gather(hidden_in, 'wide', axis=0, tiled=True).astype(jnp.float32)  41.4 us
    reduce_scatter x1, waiting for transfers between devices, shards(): lax.psum_scatter(part_q, 'narrow', scatter_dimension=0, tiled=True)  33.9 us
    dot_general x1, matrix products, shards(): part_q = jnp.dot(scaled, query_weight, preferred_element_type=jnp.float32)  15.9 us
    psum x1, blocking collectives, shards(): squares_all = lax.psum(part_sq, 'narrow')  6.44 us
    unnamed x12, local copies, waits for them, and re-layouts  5.35 us
    dot_general x1, matrix products, shards(): part_kv = jnp.dot(scaled, joint_weight, preferred_element_type=jnp.float32)  4.56 us
  transfers between devices with their start and end apart: 3, of which 2 were waited for; matrix products, arithmetic and copies ran while one was open for 15% of the time, Pallas kernels for 0%

commit v1 on v0

v1 whole, which is shorter than its diff:
```python
import functools
import math

import jax
import jax.numpy as jnp
from jax import lax
from jax.experimental import pallas as pl
from jax.experimental.pallas import tpu as pltpu
from jax.sharding import PartitionSpec as P

D = 16384
HEAD_DIM = 128
LANES = 128
MESH_ID = pl.DeviceIdType.MESH


def frequency(pair_index, head_dim):
    base = jnp.float32(500000.0) ** (-2.0 * pair_index / jnp.float32(head_dim))
    wavelen = 2.0 * math.pi / base
    smooth = (8192.0 / wavelen - 1.0) / 3.0
    middle = (1.0 - smooth) * base / 8.0 + smooth * base
    return jnp.where(wavelen < 2048.0, base, jnp.where(wavelen > 8192.0, base / 8.0, middle))


def turn(u, cosine, sine):
    lane = lax.broadcasted_iota(jnp.int32, u.shape, 1)
    other = jnp.where(lane % 2 == 0, pltpu.roll(u, LANES - 1, 1), pltpu.roll(u, 1, 1))
    return u * cosine + other * sine


def kernel(n, parts_kv, width, mid, hid, gain, cos, sin, kcos, ksin, wq, *rest):
    wkv = rest[:parts_kv]
    (out_q, out_k, out_v, raw, scaled, wq_v, wkv_v, stage_q, stage_s, got_q, got_s, own_q, own_s,
     up_sem, down_sem, in_sem, wq_sem, wkv_sem, sq_sem, ss_sem, rq_sem, rs_sem) = rest[parts_kv:]
    me = lax.axis_index("wide")
    nar = lax.axis_index("narrow")
    depth = hid.shape[1]
    chunks = wq_v.shape[0]
    kv = wkv_v.shape[1]
    key_cols = kv // 2

    def q_weight(c):
        return pltpu.make_async_copy(wq.at[:, pl.ds(pl.multiple_of(c * width, width), width)], wq_v.at[c], wq_sem.at[c])

    def kv_weight(i):
        w = kv // parts_kv
        return pltpu.make_async_copy(wkv[i], wkv_v.at[:, pl.ds(i * w, w)], wkv_sem.at[i])

    def up(blk):
        return pltpu.make_async_remote_copy(
            src_ref=raw.at[blk], dst_ref=raw.at[blk], send_sem=up_sem.at[blk], recv_sem=in_sem.at[blk],
            device_id={"wide": lax.rem(me + 1, n)}, device_id_type=MESH_ID)

    def down(blk):
        return pltpu.make_async_remote_copy(
            src_ref=raw.at[blk], dst_ref=raw.at[blk], send_sem=down_sem.at[blk], recv_sem=in_sem.at[blk],
            device_id={"wide": lax.rem(me + n - 1, n)}, device_id_type=MESH_ID)

    def send_q(blk, c):
        return pltpu.make_async_remote_copy(
            src_ref=stage_q.at[blk, c], dst_ref=got_q.at[nar, c], send_sem=sq_sem.at[blk, c],
            recv_sem=rq_sem.at[nar, c], device_id={"narrow": blk}, device_id_type=MESH_ID)

    def send_s(blk):
        return pltpu.make_async_remote_copy(
            src_ref=stage_s.at[blk], dst_ref=got_s.at[nar], send_sem=ss_sem.at[blk],
            recv_sem=rs_sem.at[nar], device_id={"narrow": blk}, device_id_type=MESH_ID)

    for i in range(parts_kv):
        kv_weight(i).start()

    @pl.loop(0, chunks)
    def _(c):
        q_weight(c).start()

    raw[me] = hid[...]
    barrier = pltpu.get_barrier_semaphore()

    @pl.when(me < n - 1)
    def _():
        pl.semaphore_signal(barrier, inc=1, device_id={"wide": lax.rem(me + 1, n)}, device_id_type=MESH_ID)

    @pl.when(me > 0)
    def _():
        pl.semaphore_signal(barrier, inc=1, device_id={"wide": lax.rem(me + n - 1, n)}, device_id_type=MESH_ID)

    for i in range(1, n):
        pl.semaphore_signal(barrier, inc=1, device_id={"narrow": lax.rem(nar + i, n)}, device_id_type=MESH_ID)
    edge = jnp.where(me > 0, 1, 0) + jnp.where(me < n - 1, 1, 0)
    pl.semaphore_wait(barrier, n - 1 + edge)

    @pl.when(me < n - 1)
    def _():
        up(me).start()

    @pl.when(me > 0)
    def _():
        down(me).start()

    def forward(d):
        low = me - d
        high = me + d

        @pl.when((low >= 0) & (me < n - 1))
        def _():
            up(low).wait_recv()
            up(low).start()

        @pl.when((high < n) & (me > 0))
        def _():
            down(high).wait_recv()
            down(high).start()

    @pl.loop(0, 2 * n - 1)
    def _(j):
        d = (j + 1) // 2
        minus = lax.rem(j, 2) == 1
        blk = jnp.where(minus, me - d, me + d)
        valid = (blk >= 0) & (blk < n)
        lead = minus | (j == 0) | (me - d < 0)

        @pl.when(valid)
        def _():
            last_here = jnp.where(minus, me == n - 1, me == 0)

            @pl.when((j > 0) & last_here)
            def _():
                up(blk).wait_recv()

            def prep(k, sq):
                for t in range(4):
                    at = pl.ds(pl.multiple_of(k * (4 * LANES) + t * LANES, LANES), LANES)
                    x = raw[blk, :, at].astype(jnp.float32)
                    scaled[:, at] = (x * gain[:, at]).astype(jnp.bfloat16)
                    sq = sq + x * x
                return sq

            rows = hid.shape[0]
            sq = lax.fori_loop(0, depth // (4 * LANES), prep, jnp.zeros((rows, LANES), jnp.float32))

            @pl.when(j == 0)
            def _():
                for i in range(parts_kv):
                    kv_weight(i).wait()

            part = jnp.dot(scaled[...], wkv_v[...], preferred_element_type=jnp.float32)
            mine = blk == nar

            @pl.when(mine)
            def _():
                own_s[:, :kv] = part
                own_s[:, kv:] = sq

            @pl.when(jnp.logical_not(mine))
            def _():
                stage_s[blk, :, :kv] = part.astype(jnp.bfloat16)
                coarse = sq.astype(jnp.bfloat16)
                stage_s[blk, :, kv:kv + LANES] = coarse
                stage_s[blk, :, kv + LANES:] = (sq - coarse.astype(jnp.float32)).astype(jnp.bfloat16)
                send_s(blk).start()

            @pl.loop(0, chunks)
            def _(c):
                @pl.when(j == 0)
                def _():
                    q_weight(c).wait()

                piece = jnp.dot(scaled[...], wq_v[c], preferred_element_type=jnp.float32)

                @pl.when(mine)
                def _():
                    own_q[c] = piece

                @pl.when(jnp.logical_not(mine))
                def _():
                    stage_q[blk, c] = piece.astype(jnp.bfloat16)
                    send_q(blk, c).start()

                @pl.when(lead & (c == mid))
                def _():
                    forward(d + 1)

    def recv_s(p):
        return pltpu.make_async_remote_copy(
            src_ref=stage_s.at[p], dst_ref=got_s.at[p], send_sem=ss_sem.at[p], recv_sem=rs_sem.at[p],
            device_id={"narrow": p}, device_id_type=MESH_ID)

    def recv_q(p, c):
        return pltpu.make_async_remote_copy(
            src_ref=stage_q.at[p, c], dst_ref=got_q.at[p, c], send_sem=sq_sem.at[p, c], recv_sem=rq_sem.at[p, c],
            device_id={"narrow": p}, device_id_type=MESH_ID)

    for i in range(1, n):
        p = lax.rem(nar + i, n)
        recv_s(p).wait_recv()
        block = got_s[p].astype(jnp.float32)
        own_s[:, :kv] += block[:, :kv]
        own_s[:, kv:] += block[:, kv:kv + LANES] + block[:, kv + LANES:]
    squares = jnp.sum(own_s[:, kv:], axis=1, keepdims=True)
    inverse = lax.rsqrt(squares / D + 1e-05)
    made = []
    for t in range(kv // LANES):
        at = slice(t * LANES, (t + 1) * LANES)
        made.append(turn(own_s[:, at] * inverse, kcos[:, at], ksin[:, at]))
    joint = jnp.concatenate(made, axis=1) if len(made) > 1 else made[0]
    out_k[...] = joint[:, :key_cols].astype(jnp.bfloat16)
    out_v[...] = joint[:, key_cols:].astype(jnp.bfloat16)

    @pl.loop(0, chunks)
    def _(c):
        for i in range(1, n):
            recv_q(lax.rem(nar + i, n), c).wait_recv()
        for t in range(width // LANES):
            at = pl.ds(t * LANES, LANES)
            u = own_q[c, :, at]
            for i in range(1, n):
                u = u + got_q[lax.rem(nar + i, n), c, :, at].astype(jnp.float32)
            turned = turn(u * inverse, cos[...], sin[...])
            out_q[:, pl.ds(pl.multiple_of(c * width + t * LANES, LANES), LANES)] = turned.astype(jnp.bfloat16)

    @pl.loop(0, n)
    def _(b):
        @pl.when((b <= me) & (me < n - 1))
        def _():
            up(b).wait_send()

        @pl.when((b >= me) & (me > 0))
        def _():
            down(b).wait_send()

    for i in range(1, n):
        b = lax.rem(nar + i, n)
        send_s(b).wait_send()

        @pl.loop(0, chunks)
        def _(c):
            send_q(b, c).wait_send()


def shards(n, hidden_in, norm_gain, query_weight, key_weight, value_weight, positions):
    rows, depth = hidden_in.shape
    query_cols = query_weight.shape[1]
    key_cols = key_weight.shape[1]
    kv = 2 * key_cols
    width = 512
    chunks = query_cols // width
    lanes = jnp.arange(HEAD_DIM, dtype=jnp.int32)
    angle = positions.astype(jnp.float32)[:, None] * frequency((lanes // 2).astype(jnp.float32), HEAD_DIM)[None, :]
    cosine = jnp.cos(angle)
    sine = jnp.where(lanes % 2 == 0, -1.0, 1.0)[None, :] * jnp.sin(angle)
    if key_cols % HEAD_DIM == 0:
        copies = key_cols // HEAD_DIM
        key_cos, key_sin = jnp.tile(cosine, (1, copies)), jnp.tile(sine, (1, copies))
        weights = (key_weight, value_weight)
    else:
        start = lax.axis_index("wide") * key_cols % HEAD_DIM
        key_cos = lax.dynamic_slice_in_dim(cosine, start, key_cols, 1)
        key_sin = lax.dynamic_slice_in_dim(sine, start, key_cols, 1)
        weights = (jnp.concatenate([key_weight, value_weight], axis=1),)
    key_cos = jnp.concatenate([key_cos, jnp.ones_like(key_cos)], axis=1)
    key_sin = jnp.concatenate([key_sin, jnp.zeros_like(key_sin)], axis=1)
    vmem = pl.BlockSpec(memory_space=pltpu.VMEM)
    hbm = pl.BlockSpec(memory_space=pl.ANY)
    bf, f32 = jnp.bfloat16, jnp.float32
    dma = pltpu.SemaphoreType.DMA
    return pl.pallas_call(
        functools.partial(kernel, n, len(weights), width, chunks * 3 // 4),
        out_shape=(
            jax.ShapeDtypeStruct((rows, query_cols), bf),
            jax.ShapeDtypeStruct((rows, key_cols), bf),
            jax.ShapeDtypeStruct((rows, key_cols), bf),
        ),
        in_specs=[vmem] * 6 + [hbm] * (1 + len(weights)),
        out_specs=(vmem, vmem, vmem),
        scratch_shapes=[
            pltpu.VMEM((n, rows, depth), bf),
            pltpu.VMEM((rows, depth), bf),
            pltpu.VMEM((chunks, depth, width), bf),
            pltpu.VMEM((depth, kv), bf),
            pltpu.VMEM((n, chunks, rows, width), bf),
            pltpu.VMEM((n, rows, kv + 2 * LANES), bf),
            pltpu.VMEM((n, chunks, rows, width), bf),
            pltpu.VMEM((n, rows, kv + 2 * LANES), bf),
            pltpu.VMEM((chunks, rows, width), f32),
            pltpu.VMEM((rows, kv + LANES), f32),
            dma((n,)), dma((n,)), dma((n,)),
            dma((chunks,)), dma((len(weights),)),
            dma((n, chunks)), dma((n,)),
            dma((n, chunks)), dma((n,)),
        ],
        compiler_params=pltpu.CompilerParams(
            collective_id=0, has_side_effects=True, vmem_limit_bytes=58 * 1024 * 1024),
        cost_estimate=pl.CostEstimate(
            flops=2 * n * rows * depth * (query_cols + kv),
            bytes_accessed=2 * depth * (query_cols + kv), transcendentals=0),
    )(hidden_in, norm_gain[None, :], cosine, sine, key_cos, key_sin, query_weight, *weights)


def solution(mesh):
    n = mesh.shape["narrow"]
    assert mesh.shape["wide"] == n
    return jax.shard_map(
        functools.partial(shards, n),
        mesh=mesh,
        in_specs=(
            P(("grp", "wide"), "narrow"),
            P("narrow"),
            P("narrow", "wide"),
            P("narrow", "wide"),
            P("narrow", "wide"),
            P(("grp", "narrow")),
        ),
        out_specs=(
            P(("grp", "narrow"), "wide"),
            P(("grp", "narrow"), "wide"),
            P(("grp", "narrow"), "wide"),
        ),
        check_vma=False,
    )
```

time: 132 us -> 56.4 us (0.43)
  waiting for transfers between devices: 76 us -> 0 us
  Pallas kernels: 0 us -> 48 us
  matrix products: 20.4 us -> 0 us
  between operations: 13.9 us -> 0.69 us
  blocking collectives: 6.44 us -> 0 us
  other arithmetic: 5.28 us -> 0.85 us
  local copies, waits for them, and re-layouts: 9.47 us -> 5.82 us
    pallas_call x0 -> x1, Pallas kernels: none -> 48 us  [shards(): pl.pallas_call(functools.partial(kernel, n, len(weights), width, chunks *...]
    all_gather x1 -> x0, waiting for transfers between devices: 41.4 us -> none  [shards(): lax.all_gather(hidden_in, 'wide', axis=0, tiled=True).astype(jnp.float32)]
    reduce_scatter x2 -> x0, waiting for transfers between devices: 33.9 us -> none  [the longest x1 33.9 us: shards(): lax.psum_scatter(part_q, 'narrow', scatter_dimension=0, tiled=True)]
    dot_general x2 -> x0, matrix products: 20.4 us -> none  [the longest x1 15.9 us: shards(): part_q = jnp.dot(scaled, query_weight, preferred_element_type=jnp.float32)]
    psum x1 -> x0, blocking collectives: 6.44 us -> none  [shards(): squares_all = lax.psum(part_sq, 'narrow')]
    slice x2 -> x0, local copies, waits for them, and re-layouts: 2.55 us -> none  [rotate(): second = pairs[:, :, 1]]
    another operation x4 -> x0, other arithmetic: 1.96 us -> none
    unnamed x12 -> x9, local copies, waits for them, and re-layouts: 5.35 us -> 4.48 us
  transfers between devices with their start and end apart: 3 -> 0, of which waited for: 2 -> 0; matrix products, arithmetic and copies ran while one was open for 15% -> 0% of each run, Pallas kernels for 0% -> 0%
where the time goes in v1:
time: 56.4 us; the launch traced here: 55.3 us
  Pallas kernels  48 us (85%)
  local copies, waits for them, and re-layouts  5.82 us (10%)
  other arithmetic  0.85 us (2%)
  between operations  0.69 us (1%)
    pallas_call x1, Pallas kernels, shards(): pl.pallas_call(functools.partial(kernel, n, len(weights), width, chunks *...  48 us
    unnamed x9, local copies, waits for them, and re-layouts  4.48 us

profile of v1, /device:TPU:0, one launch (start us, length us, event | category | flops | bytes accessed | tf_op | source)
XLA Modules:
  0.0 55.3 jit_solution(12345545775163531032)
XLA Ops:
  0.6 0.7 %convert_element_type.10 = f32[48]{0:T(128)S(1)} convert(s32[48]{0:T(128)} %param.11) | non-fusion elementwise | flops 48 | bytes 384 | tf_op jit(solution)/shard_map/convert_element_type | solution.py:248
  1.3 0.2 fusion
  1.5 0.0 copy-start
  1.5 0.0 copy-start.1
  1.6 0.7 %concatenate.7.ksin = f32[48,512]{1,0:T(8,128)} pad(f32[48,256]{1,0:T(8,128)S(1)} %bitcast.11, f32[]{:T(128)} %constant.58.clone.1), padding=0_0x0_256 | pad | bytes 147460 | tf_op jit(solution)/shard_map/concatenate | solution.py:261
  2.2 0.6 %concatenate.6.kcos = f32[48,512]{1,0:T(8,128)} pad(f32[48,256]{1,0:T(8,128)S(1)} %bitcast.12, f32[]{:T(128)} %constant.54.clone.1), padding=0_0x0_256 | pad | bytes 147460 | tf_op jit(solution)/shard_map/concatenate | solution.py:260
  2.9 0.0 copy-done
  2.9 0.0 copy-done.1
  2.9 48.0 %shard_map.85 = (bf16[48,4096]{1,0:T(8,128)(2,1)}, bf16[48,256]{1,0:T(8,128)(2,1)}, bf16[48,256]{1,0:T(8,128)(2,1)}) custom-call(bf16[48,4096]{1,0:T(8,128)(2,1)} %hid.1, f32[1,4096]{1,0:T(1,128)} %bitcast.13, f32[48,128]{1,0:T(8,128)} %copy-done.1, f32[48,128]{1,0:T(8,128)} %copy-done, f32[48,512]{1,0:T(8,128)} %concatenate.6.kcos, ...), custom_call_target="tpu_custom_call" | custom-call | flops 7247757312 | bytes 37748736 | tf_op jit(solution)/shard_map/pallas_call | solution.py:266
  50.9 1.8 %copy.18 = bf16[48,4096]{1,0:T(8,128)(2,1)} copy(bf16[48,4096]{1,0:T(8,128)(2,1)} %get-tuple-element.10) | data formatting | bytes 786432
  52.6 1.3 %copy.19 = bf16[48,256]{1,0:T(8,128)(2,1)} copy(bf16[48,256]{1,0:T(8,128)(2,1)} %get-tuple-element.11) | data formatting | bytes 49152
  54.0 1.3 %copy.20 = bf16[48,256]{1,0:T(8,128)(2,1)} copy(bf16[48,256]{1,0:T(8,128)(2,1)} %get-tuple-element.12) | data formatting | bytes 49152
  (5 shorter events, 0.1 us)
Async XLA Ops:
  1.5 1.4 %copy-start = (f32[48,128]{1,0:T(8,128)}, f32[48,128]{1,0:T(8,128)S(1)}, u32[]{:S(2)}) copy-start(f32[48,128]{1,0:T(8,128)S(1)} %get-tuple-element.3.sin) | copy-start | bytes 73732
  1.5 1.4 %copy-start.1 = (f32[48,128]{1,0:T(8,128)}, f32[48,128]{1,0:T(8,128)S(1)}, u32[]{:S(2)}) copy-start(f32[48,128]{1,0:T(8,128)S(1)} %get-tuple-element.4.cos) | copy-start | bytes 73732

commit v2 on v1

--- a/solution.py
+++ b/solution.py
@@ -28,7 +28,9 @@
     return u * cosine + other * sine
 
 
-def kernel(n, parts_kv, width, mid, hid, gain, cos, sin, kcos, ksin, wq, *rest):
+def kernel(n, parts_kv, width, pieces, points, aligned, hid, gain, cos, sin, *rest):
+    tables = rest[:0 if aligned else 2]
+    wq, rest = rest[len(tables)], rest[len(tables) + 1:]
     wkv = rest[:parts_kv]
     (out_q, out_k, out_v, raw, scaled, wq_v, wkv_v, stage_q, stage_s, got_q, got_s, own_q, own_s,
      up_sem, down_sem, in_sem, wq_sem, wkv_sem, sq_sem, ss_sem, rq_sem, rs_sem) = rest[parts_kv:]
@@ -46,14 +48,14 @@
         w = kv // parts_kv
         return pltpu.make_async_copy(wkv[i], wkv_v.at[:, pl.ds(i * w, w)], wkv_sem.at[i])
 
-    def up(blk):
-        return pltpu.make_async_remote_copy(
-            src_ref=raw.at[blk], dst_ref=raw.at[blk], send_sem=up_sem.at[blk], recv_sem=in_sem.at[blk],
+    def up(blk, h):
+        return pltpu.make_async_remote_copy(
+            src_ref=raw.at[blk, h], dst_ref=raw.at[blk, h], send_sem=up_sem.at[blk, h], recv_sem=in_sem.at[blk, h],
             device_id={"wide": lax.rem(me + 1, n)}, device_id_type=MESH_ID)
 
-    def down(blk):
-        return pltpu.make_async_remote_copy(
-            src_ref=raw.at[blk], dst_ref=raw.at[blk], send_sem=down_sem.at[blk], recv_sem=in_sem.at[blk],
+    def down(blk, h):
+        return pltpu.make_async_remote_copy(
+            src_ref=raw.at[blk, h], dst_ref=raw.at[blk, h], send_sem=down_sem.at[blk, h], recv_sem=in_sem.at[blk, h],
             device_id={"wide": lax.rem(me + n - 1, n)}, device_id_type=MESH_ID)
 
     def send_q(blk, c):
@@ -73,7 +75,9 @@
     def _(c):
         q_weight(c).start()
 
-    raw[me] = hid[...]
+    cut = depth // pieces
+    for h in range(pieces):
+        raw[me, h] = hid[:, h * cut:(h + 1) * cut]
     barrier = pltpu.get_barrier_semaphore()
 
     @pl.when(me < n - 1)
@@ -91,25 +95,27 @@
 
     @pl.when(me < n - 1)
     def _():
-        up(me).start()
+        for h in range(pieces):
+            up(me, h).start()
 
     @pl.when(me > 0)
     def _():
-        down(me).start()
-
-    def forward(d):
+        for h in range(pieces):
+            down(me, h).start()
+
+    def forward(d, h):
         low = me - d
         high = me + d
 
         @pl.when((low >= 0) & (me < n - 1))
         def _():
-            up(low).wait_recv()
-            up(low).start()
+            up(low, h).wait_recv()
+            up(low, h).start()
 
         @pl.when((high < n) & (me > 0))
         def _():
-            down(high).wait_recv()
-            down(high).start()
+            down(high, h).wait_recv()
+            down(high, h).start()
 
     @pl.loop(0, 2 * n - 1)
     def _(j):
@@ -125,18 +131,22 @@
 
             @pl.when((j > 0) & last_here)
             def _():
-                up(blk).wait_recv()
-
-            def prep(k, sq):
-                for t in range(4):
+                for h in range(pieces):
+                    up(blk, h).wait_recv()
+
+            def prep(k, sq, h):
+                for t in range(min(4, cut // LANES)):
                     at = pl.ds(pl.multiple_of(k * (4 * LANES) + t * LANES, LANES), LANES)
-                    x = raw[blk, :, at].astype(jnp.float32)
-                    scaled[:, at] = (x * gain[:, at]).astype(jnp.bfloat16)
+                    x = raw[blk, h, :, at].astype(jnp.float32)
+                    to = pl.ds(pl.multiple_of(h * cut + k * (4 * LANES) + t * LANES, LANES), LANES)
+                    scaled[:, to] = (x * gain[:, to]).astype(jnp.bfloat16)
                     sq = sq + x * x
                 return sq
 
             rows = hid.shape[0]
-            sq = lax.fori_loop(0, depth // (4 * LANES), prep, jnp.zeros((rows, LANES), jnp.float32))
+            sq = jnp.zeros((rows, LANES), jnp.float32)
+            for h in range(pieces):
+                sq = lax.fori_loop(0, max(1, cut // (4 * LANES)), functools.partial(prep, h=h), sq)
 
             @pl.when(j == 0)
             def _():
@@ -176,9 +186,10 @@
                     stage_q[blk, c] = piece.astype(jnp.bfloat16)
                     send_q(blk, c).start()
 
-                @pl.when(lead & (c == mid))
-                def _():
-                    forward(d + 1)
+                for h in range(pieces):
+                    @pl.when(lead & (c == jnp.where(j == 0, points[0][h], points[1][h])))
+                    def _():
+                        forward(d + 1, h)
 
     def recv_s(p):
         return pltpu.make_async_remote_copy(
@@ -201,7 +212,12 @@
     made = []
     for t in range(kv // LANES):
         at = slice(t * LANES, (t + 1) * LANES)
-        made.append(turn(own_s[:, at] * inverse, kcos[:, at], ksin[:, at]))
+        u = own_s[:, at] * inverse
+        if not aligned:
+            u = turn(u, tables[0][:, at], tables[1][:, at])
+        elif t * LANES < key_cols:
+            u = turn(u, cos[...], sin[...])
+        made.append(u)
     joint = jnp.concatenate(made, axis=1) if len(made) > 1 else made[0]
     out_k[...] = joint[:, :key_cols].astype(jnp.bfloat16)
     out_v[...] = joint[:, key_cols:].astype(jnp.bfloat16)
@@ -222,11 +238,13 @@
     def _(b):
         @pl.when((b <= me) & (me < n - 1))
         def _():
-            up(b).wait_send()
+            for h in range(pieces):
+                up(b, h).wait_send()
 
         @pl.when((b >= me) & (me > 0))
         def _():
-            down(b).wait_send()
+            for h in range(pieces):
+                down(b, h).wait_send()
 
     for i in range(1, n):
         b = lax.rem(nar + i, n)
@@ -235,6 +253,11 @@
         @pl.loop(0, chunks)
         def _(c):
             send_q(b, c).wait_send()
+
+
+def hand_over(*refs):
+    for i in range(3):
+        refs[3 + i][...] = refs[i][...]
 
 
 def shards(n, hidden_in, norm_gain, query_weight, key_weight, value_weight, positions):
@@ -249,31 +272,33 @@
     cosine = jnp.cos(angle)
     sine = jnp.where(lanes % 2 == 0, -1.0, 1.0)[None, :] * jnp.sin(angle)
     if key_cols % HEAD_DIM == 0:
-        copies = key_cols // HEAD_DIM
-        key_cos, key_sin = jnp.tile(cosine, (1, copies)), jnp.tile(sine, (1, copies))
+        tables = ()
         weights = (key_weight, value_weight)
     else:
         start = lax.axis_index("wide") * key_cols % HEAD_DIM
         key_cos = lax.dynamic_slice_in_dim(cosine, start, key_cols, 1)
         key_sin = lax.dynamic_slice_in_dim(sine, start, key_cols, 1)
         weights = (jnp.concatenate([key_weight, value_weight], axis=1),)
-    key_cos = jnp.concatenate([key_cos, jnp.ones_like(key_cos)], axis=1)
-    key_sin = jnp.concatenate([key_sin, jnp.zeros_like(key_sin)], axis=1)
+        key_cos = jnp.concatenate([key_cos, jnp.ones_like(key_cos)], axis=1)
+        key_sin = jnp.concatenate([key_sin, jnp.zeros_like(key_sin)], axis=1)
+        tables = (key_cos, key_sin)
     vmem = pl.BlockSpec(memory_space=pltpu.VMEM)
     hbm = pl.BlockSpec(memory_space=pl.ANY)
     bf, f32 = jnp.bfloat16, jnp.float32
     dma = pltpu.SemaphoreType.DMA
-    return pl.pallas_call(
-        functools.partial(kernel, n, len(weights), width, chunks * 3 // 4),
+    pieces = 2
+    points = tuple(tuple(p * chunks // 8 for p in at) for at in ((2, 6), (3, 7)))
+    results = pl.pallas_call(
+        functools.partial(kernel, n, len(weights), width, pieces, points, not tables),
         out_shape=(
             jax.ShapeDtypeStruct((rows, query_cols), bf),
             jax.ShapeDtypeStruct((rows, key_cols), bf),
             jax.ShapeDtypeStruct((rows, key_cols), bf),
         ),
-        in_specs=[vmem] * 6 + [hbm] * (1 + len(weights)),
+        in_specs=[vmem] * (4 + len(tables)) + [hbm] * (1 + len(weights)),
         out_specs=(vmem, vmem, vmem),
         scratch_shapes=[
-            pltpu.VMEM((n, rows, depth), bf),
+            pltpu.VMEM((n, pieces, rows, depth // pieces), bf),
             pltpu.VMEM((rows, depth), bf),
             pltpu.VMEM((chunks, depth, width), bf),
             pltpu.VMEM((depth, kv), bf),
@@ -283,7 +308,7 @@
             pltpu.VMEM((n, rows, kv + 2 * LANES), bf),
             pltpu.VMEM((chunks, rows, width), f32),
             pltpu.VMEM((rows, kv + LANES), f32),
-            dma((n,)), dma((n,)), dma((n,)),
+            dma((n, pieces)), dma((n, pieces)), dma((n, pieces)),
             dma((chunks,)), dma((len(weights),)),
             dma((n, chunks)), dma((n,)),
             dma((n, chunks)), dma((n,)),
@@ -293,7 +318,13 @@
         cost_estimate=pl.CostEstimate(
             flops=2 * n * rows * depth * (query_cols + kv),
             bytes_accessed=2 * depth * (query_cols + kv), transcendentals=0),
-    )(hidden_in, norm_gain[None, :], cosine, sine, key_cos, key_sin, query_weight, *weights)
+    )(hidden_in, norm_gain[None, :], cosine, sine, *tables, query_weight, *weights)
+    return pl.pallas_call(
+        hand_over,
+        out_shape=tuple(jax.ShapeDtypeStruct(x.shape, x.dtype) for x in results),
+        in_specs=[vmem] * 3,
+        out_specs=(vmem,) * 3,
+    )(*results)
 
 
 def solution(mesh):

time: 56.4 us -> 51.3 us (0.910)
  local copies, waits for them, and re-layouts: 5.82 us -> 0 us
  other arithmetic: 0.85 us -> 1.48 us
    unnamed x9 -> x0, local copies, waits for them, and re-layouts: 4.48 us -> none
    concatenate x2 -> x0, local copies, waits for them, and re-layouts: 1.3 us -> none  [the longest x1 0.66 us: shards(): key_sin = jnp.concatenate([key_sin, jnp.zeros_like(key_sin)], axis=1)]
    mul x1, other arithmetic: 0.18 us -> 0.8 us  [shards(): sine = jnp.where(lanes % 2 == 0, -1.0, 1.0)[None, :] * jnp.sin(angle)]
    pallas_call x1 -> x2, Pallas kernels: 48 us -> 48.3 us  [the longest x1 46.5 us: shards(): pl.pallas_call(functools.partial(kernel, n, len(weights), width, pieces,...]
where the time goes in v2:
time: 51.3 us; the launch traced here: 50.4 us
  Pallas kernels  48.3 us (94%)
  other arithmetic  1.48 us (3%)
  between operations  0.64 us (1%)
    pallas_call x1, Pallas kernels, shards(): pl.pallas_call(functools.partial(kernel, n, len(weights), width, pieces,...  46.5 us
    pallas_call x1, Pallas kernels, shards(): pl.pallas_call(hand_over, out_shape=tuple((jax.ShapeDtypeStruct(x.shape,...  1.79 us

profile of v2, /device:TPU:0, one launch (start us, length us, event | category | flops | bytes accessed | tf_op | source)
XLA Modules:
  0.0 50.4 jit_solution(3078660321378234163)
XLA Ops:
  0.6 0.7 %convert_element_type.10 = f32[48]{0:T(128)S(1)} convert(s32[48]{0:T(128)} %param.11) | non-fusion elementwise | flops 48 | bytes 384 | tf_op jit(solution)/shard_map/convert_element_type | solution.py:271
  1.3 0.8 %fusion = (f32[48,128]{1,0:T(8,128)}, f32[48,128]{1,0:T(8,128)}) fusion(f32[128]{0:T(128)S(1)} %get-tuple-element.11, f32[128]{0:T(128)S(1)} %get-tuple-element.12, f32[48]{0:T(128)S(1)} %convert_element_type.10), kind=kLoop, calls=%fused_computation.2 | loop fusion | flops 12288 | bytes 50368 | tf_op jit(solution)/shard_map/mul | solution.py:273
  2.1 46.5 %shard_map.85 = (bf16[48,4096]{1,0:T(8,128)(2,1)}, bf16[48,256]{1,0:T(8,128)(2,1)}, bf16[48,256]{1,0:T(8,128)(2,1)}) custom-call(bf16[48,4096]{1,0:T(8,128)(2,1)} %hid.1, f32[1,4096]{1,0:T(1,128)} %bitcast.1, f32[48,128]{1,0:T(8,128)} %get-tuple-element.10.cos, f32[48,128]{1,0:T(8,128)} %get-tuple-element.9.sin, bf16[4096,4096]{1,0:T(8,128)(2,1)} %rest_0_.1, ...), custom_call_target="tpu_custom_call" | custom-call | flops 7247757312 | bytes 37748736 | tf_op jit(solution)/shard_map/pallas_call | solution.py:291
  48.6 1.8 %shard_map.86 = (bf16[48,4096]{1,0:T(8,128)(2,1)}, bf16[48,256]{1,0:T(8,128)(2,1)}, bf16[48,256]{1,0:T(8,128)(2,1)}) custom-call(bf16[48,4096]{1,0:T(8,128)(2,1)} %get-tuple-element.6.refs_0_, bf16[48,256]{1,0:T(8,128)(2,1)} %get-tuple-element.7.refs_1_, bf16[48,256]{1,0:T(8,128)(2,1)} %get-tuple-element.8.refs_2_), custom_call_target="tpu_custom_call" | custom-call | tf_op jit(solution)/shard_map/pallas_call | solution.py:322
  (1 shorter events, 0.0 us)

commit v3 on v2

--- a/solution.py
+++ b/solution.py
@@ -32,8 +32,8 @@
     tables = rest[:0 if aligned else 2]
     wq, rest = rest[len(tables)], rest[len(tables) + 1:]
     wkv = rest[:parts_kv]
-    (out_q, out_k, out_v, raw, scaled, wq_v, wkv_v, stage_q, stage_s, got_q, got_s, own_q, own_s,
-     up_sem, down_sem, in_sem, wq_sem, wkv_sem, sq_sem, ss_sem, rq_sem, rs_sem) = rest[parts_kv:]
+    (out_q, out_k, out_v, raw, scaled, wq_v, wkv_v, stage_q, stage_s, got_q, pair_q, got_s, own_q, own_s,
+     up_sem, down_sem, in_sem, wq_sem, wkv_sem, sq_sem, pq_sem, ss_sem, rq_sem, rs_sem) = rest[parts_kv:]
     me = lax.axis_index("wide")
     nar = lax.axis_index("narrow")
     depth = hid.shape[1]
@@ -62,6 +62,21 @@
         return pltpu.make_async_remote_copy(
             src_ref=stage_q.at[blk, c], dst_ref=got_q.at[nar, c], send_sem=sq_sem.at[blk, c],
             recv_sem=rq_sem.at[nar, c], device_id={"narrow": blk}, device_id_type=MESH_ID)
+
+    core = lax.rem(nar, 2)
+    chip = nar // 2
+    buddy = nar + 1 - 2 * core
+
+    def swap_q(blk, c):
+        return pltpu.make_async_remote_copy(
+            src_ref=stage_q.at[blk, c], dst_ref=pair_q.at[blk, c], send_sem=sq_sem.at[blk, c],
+            recv_sem=pq_sem.at[blk, c], device_id={"narrow": buddy}, device_id_type=MESH_ID)
+
+    def combine(blk, c):
+        swap_q(blk, c).wait_recv()
+        both = stage_q[blk, c].astype(jnp.float32) + pair_q[blk, c].astype(jnp.float32)
+        stage_q[blk, c] = both.astype(jnp.bfloat16)
+        send_q(blk, c).start()
 
     def send_s(blk):
         return pltpu.make_async_remote_copy(
@@ -184,12 +199,27 @@
                 @pl.when(jnp.logical_not(mine))
                 def _():
                     stage_q[blk, c] = piece.astype(jnp.bfloat16)
+
+                @pl.when(blk == buddy)
+                def _():
                     send_q(blk, c).start()
+
+                @pl.when((blk // 2 != chip) & (lax.rem(c, 2) != core))
+                def _():
+                    swap_q(blk, c).start()
+
+                    @pl.when(c > 0)
+                    def _():
+                        combine(blk, c - 1)
 
                 for h in range(pieces):
                     @pl.when(lead & (c == jnp.where(j == 0, points[0][h], points[1][h])))
                     def _():
                         forward(d + 1, h)
+
+            @pl.when((blk // 2 != chip) & (lax.rem(chunks - 1, 2) == core))
+            def _():
+                combine(blk, chunks - 1)
 
     def recv_s(p):
         return pltpu.make_async_remote_copy(
@@ -224,13 +254,16 @@
 
     @pl.loop(0, chunks)
     def _(c):
-        for i in range(1, n):
-            recv_q(lax.rem(nar + i, n), c).wait_recv()
+        sources = [buddy]
+        for i in range(1, n // 2):
+            sources.append(2 * lax.rem(chip + i, n // 2) + lax.rem(c, 2))
+        for p in sources:
+            recv_q(p, c).wait_recv()
         for t in range(width // LANES):
             at = pl.ds(t * LANES, LANES)
             u = own_q[c, :, at]
-            for i in range(1, n):
-                u = u + got_q[lax.rem(nar + i, n), c, :, at].astype(jnp.float32)
+            for p in sources:
+                u = u + got_q[p, c, :, at].astype(jnp.float32)
             turned = turn(u * inverse, cos[...], sin[...])
             out_q[:, pl.ds(pl.multiple_of(c * width + t * LANES, LANES), LANES)] = turned.astype(jnp.bfloat16)
 
@@ -305,12 +338,13 @@
             pltpu.VMEM((n, chunks, rows, width), bf),
             pltpu.VMEM((n, rows, kv + 2 * LANES), bf),
             pltpu.VMEM((n, chunks, rows, width), bf),
+            pltpu.VMEM((n, chunks, rows, width), bf),
             pltpu.VMEM((n, rows, kv + 2 * LANES), bf),
             pltpu.VMEM((chunks, rows, width), f32),
             pltpu.VMEM((rows, kv + LANES), f32),
             dma((n, pieces)), dma((n, pieces)), dma((n, pieces)),
             dma((chunks,)), dma((len(weights),)),
-            dma((n, chunks)), dma((n,)),
+            dma((n, chunks)), dma((n, chunks)), dma((n,)),
             dma((n, chunks)), dma((n,)),
         ],
         compiler_params=pltpu.CompilerParams(

time: 51.3 us -> 50.2 us (0.979)
  Pallas kernels: 48.3 us -> 47.5 us
    pallas_call x1, Pallas kernels: 46.5 us -> 45.7 us  [shards(): pl.pallas_call(functools.partial(kernel, n, len(weights), width, pieces,...]
where the time goes in v3:
time: 50.2 us; the launch traced here: 49.6 us
  Pallas kernels  47.5 us (95%)
  other arithmetic  1.48 us (3%)
  between operations  0.64 us (1%)
    pallas_call x1, Pallas kernels, shards(): pl.pallas_call(functools.partial(kernel, n, len(weights), width, pieces,...  45.7 us
    pallas_call x1, Pallas kernels, shards(): pl.pallas_call(hand_over, out_shape=tuple((jax.ShapeDtypeStruct(x.shape,...  1.79 us

profile of v3, /device:TPU:0, one launch (start us, length us, event | category | flops | bytes accessed | tf_op | source)
XLA Modules:
  0.0 49.6 jit_solution(13307297782401317464)
XLA Ops:
  0.6 0.7 %convert_element_type.10 = f32[48]{0:T(128)S(1)} convert(s32[48]{0:T(128)} %param.11) | non-fusion elementwise | flops 48 | bytes 384 | tf_op jit(solution)/shard_map/convert_element_type | solution.py:304
  1.3 0.8 %fusion = (f32[48,128]{1,0:T(8,128)}, f32[48,128]{1,0:T(8,128)}) fusion(f32[128]{0:T(128)S(1)} %get-tuple-element.11, f32[128]{0:T(128)S(1)} %get-tuple-element.12, f32[48]{0:T(128)S(1)} %convert_element_type.10), kind=kLoop, calls=%fused_computation.2 | loop fusion | flops 12288 | bytes 50368 | tf_op jit(solution)/shard_map/mul | solution.py:306
  2.1 45.7 %shard_map.85 = (bf16[48,4096]{1,0:T(8,128)(2,1)}, bf16[48,256]{1,0:T(8,128)(2,1)}, bf16[48,256]{1,0:T(8,128)(2,1)}) custom-call(bf16[48,4096]{1,0:T(8,128)(2,1)} %hid.1, f32[1,4096]{1,0:T(1,128)} %bitcast.1, f32[48,128]{1,0:T(8,128)} %get-tuple-element.10.cos, f32[48,128]{1,0:T(8,128)} %get-tuple-element.9.sin, bf16[4096,4096]{1,0:T(8,128)(2,1)} %rest_0_.1, ...), custom_call_target="tpu_custom_call" | custom-call | flops 7247757312 | bytes 37748736 | tf_op jit(solution)/shard_map/pallas_call | solution.py:324
  47.8 1.8 %shard_map.86 = (bf16[48,4096]{1,0:T(8,128)(2,1)}, bf16[48,256]{1,0:T(8,128)(2,1)}, bf16[48,256]{1,0:T(8,128)(2,1)}) custom-call(bf16[48,4096]{1,0:T(8,128)(2,1)} %get-tuple-element.6.refs_0_, bf16[48,256]{1,0:T(8,128)(2,1)} %get-tuple-element.7.refs_1_, bf16[48,256]{1,0:T(8,128)(2,1)} %get-tuple-element.8.refs_2_), custom_call_target="tpu_custom_call" | custom-call | tf_op jit(solution)/shard_map/pallas_call | solution.py:356
  (1 shorter events, 0.0 us)

commit v4 on v3

--- a/solution.py
+++ b/solution.py
@@ -298,7 +298,7 @@
     query_cols = query_weight.shape[1]
     key_cols = key_weight.shape[1]
     kv = 2 * key_cols
-    width = 512
+    width = min(1024, query_cols)
     chunks = query_cols // width
     lanes = jnp.arange(HEAD_DIM, dtype=jnp.int32)
     angle = positions.astype(jnp.float32)[:, None] * frequency((lanes // 2).astype(jnp.float32), HEAD_DIM)[None, :]

time: 50.2 us -> 48.7 us (0.970)
  Pallas kernels: 47.5 us -> 45.7 us
    pallas_call x1, Pallas kernels: 45.7 us -> 43.9 us  [shards(): pl.pallas_call(functools.partial(kernel, n, len(weights), width, pieces,...]
where the time goes in v4:
time: 48.7 us; the launch traced here: 47.8 us
  Pallas kernels  45.7 us (94%)
  other arithmetic  1.48 us (3%)
  between operations  0.64 us (1%)
    pallas_call x1, Pallas kernels, shards(): pl.pallas_call(functools.partial(kernel, n, len(weights), width, pieces,...  43.9 us
    pallas_call x1, Pallas kernels, shards(): pl.pallas_call(hand_over, out_shape=tuple((jax.ShapeDtypeStruct(x.shape,...  1.79 us

profile of v4, /device:TPU:0, one launch (start us, length us, event | category | flops | bytes accessed | tf_op | source)
XLA Modules:
  0.0 47.8 jit_solution(6361395162805461084)
XLA Ops:
  0.6 0.7 %convert_element_type.10 = f32[48]{0:T(128)S(1)} convert(s32[48]{0:T(128)} %param.11) | non-fusion elementwise | flops 48 | bytes 384 | tf_op jit(solution)/shard_map/convert_element_type | solution.py:304
  1.3 0.8 %fusion = (f32[48,128]{1,0:T(8,128)}, f32[48,128]{1,0:T(8,128)}) fusion(f32[128]{0:T(128)S(1)} %get-tuple-element.11, f32[128]{0:T(128)S(1)} %get-tuple-element.12, f32[48]{0:T(128)S(1)} %convert_element_type.10), kind=kLoop, calls=%fused_computation.2 | loop fusion | flops 12288 | bytes 50368 | tf_op jit(solution)/shard_map/mul | solution.py:306
  2.1 43.9 %shard_map.85 = (bf16[48,4096]{1,0:T(8,128)(2,1)}, bf16[48,256]{1,0:T(8,128)(2,1)}, bf16[48,256]{1,0:T(8,128)(2,1)}) custom-call(bf16[48,4096]{1,0:T(8,128)(2,1)} %hid.1, f32[1,4096]{1,0:T(1,128)} %bitcast.1, f32[48,128]{1,0:T(8,128)} %get-tuple-element.10.cos, f32[48,128]{1,0:T(8,128)} %get-tuple-element.9.sin, bf16[4096,4096]{1,0:T(8,128)(2,1)} %rest_0_.1, ...), custom_call_target="tpu_custom_call" | custom-call | flops 7247757312 | bytes 37748736 | tf_op jit(solution)/shard_map/pallas_call | solution.py:324
  46.0 1.8 %shard_map.86 = (bf16[48,4096]{1,0:T(8,128)(2,1)}, bf16[48,256]{1,0:T(8,128)(2,1)}, bf16[48,256]{1,0:T(8,128)(2,1)}) custom-call(bf16[48,4096]{1,0:T(8,128)(2,1)} %get-tuple-element.6.refs_0_, bf16[48,256]{1,0:T(8,128)(2,1)} %get-tuple-element.7.refs_1_, bf16[48,256]{1,0:T(8,128)(2,1)} %get-tuple-element.8.refs_2_), custom_call_target="tpu_custom_call" | custom-call | tf_op jit(solution)/shard_map/pallas_call | solution.py:356
  (1 shorter events, 0.0 us)
